TPU v7x, 32 devices: a whole 2x2x4 slice. The times are simulated.
32 devices in a mesh: mem: 4 (over y, x), dom: 8 (over z, core).
Axes of the slice: x: 2, y: 2, z: 4, core: 2. Of those that a mesh axis runs over, the one named last changes fastest.
Arguments:
- state: bfloat16 [64, 6, 4, 256, 128], P('mem', None, None, 'dom'), may hold values from -6 to 6
- wind_x: float32 [4, 256, 128], P(None, 'dom'), may hold values from -0.5 to 0.5
- wind_y: float32 [4, 256, 128], P(None, 'dom'), may hold values from -0.5 to 0.5
- viscosity_numbers: float32 [6], replicated, may hold values from 0.02 to 0.2
- weights: float32 [256, 64, 64], P('dom'), may hold values from -0.75 to 0.75
- obs_count: int32 [256], replicated, may hold values from 0 to 45, as said below
- owner: int32 [256], replicated, may hold values from 0 to 7, as said below
Outputs:
- analysis: bfloat16 [64, 6, 4, 256, 128], P('mem', None, None, 'dom')
Inputs may be any that keep to these rules, and one draw needn't show every extreme that they name: `obs_count`: block 0 has 45 observations. `owner`: each device's blocks, ranked by falling observation count (ties by position), are dealt to owners in turn, so that every device owns exactly 4 of each device's 32 blocks.
All inputs are finite; a program needn't handle non-finite values.
Results may differ from a plain program's by a relative error of at most 0.007.
Values may be sent and summed in bfloat16 or wider, within the bound.
A program may use at most 64 MiB of HBM per device.

v0:
```python
import jax
import jax.numpy as jnp
from jax import lax
from jax.sharding import PartitionSpec as P

OBS_HALF = 8


def with_halo(block, sides, width):
    for axis, dim in sides:
        count = lax.axis_size(axis)
        forward = [(i, i + 1) for i in range(count - 1)]
        backward = [(target, source) for source, target in forward]
        low = lax.ppermute(
            lax.slice_in_dim(block, block.shape[dim] - width, None, axis=dim), axis, forward
        )
        high = lax.ppermute(lax.slice_in_dim(block, 0, width, axis=dim), axis, backward)
        block = jnp.concatenate([low, block, high], axis=dim)
    return block


def combined(weight, counts):
    number = counts.astype(jnp.float32)
    gain = number / (number + OBS_HALF)
    eye = jnp.eye(weight.shape[-1], dtype=jnp.float32)
    transform_weights_square = (1.0 - gain)[:, None, None] * eye + gain[:, None, None] * weight
    return (
        transform_weights_square
        - jnp.mean(transform_weights_square, axis=1, keepdims=True)
        + 1.0 / weight.shape[-1]
    ).astype(jnp.bfloat16)


def per_device(state, wind_x, wind_y, viscosity_numbers, weights, obs_count, owner):
    member_total = lax.axis_size("mem")
    n_dom = lax.axis_size("dom")
    members_on_shard, field_stack, levels, row_block, grid_cells = state.shape
    members = members_on_shard * member_total
    quarter_part = levels // member_total
    per_owner = row_block // n_dom
    here = lax.axis_index("dom")
    padded = with_halo(state, (("dom", 3),), 1).astype(jnp.float32)
    middle_part = padded[:, :, :, 1:-1, :]
    upper = padded[:, :, :, 2:, :]
    lower = padded[:, :, :, :-2, :]
    side_pad = jnp.pad(middle_part, ((0, 0), (0, 0), (0, 0), (0, 0), (1, 1)))
    east = side_pad[..., 2:]
    west = side_pad[..., :-2]
    ensemble_spread = upper + lower + east + west - 4.0 * middle_part
    carried_along = wind_x * (east - west) + wind_y * (upper - lower)
    predicted_prior = (
        middle_part + viscosity_numbers[:, None, None, None] * ensemble_spread - 0.5 * carried_along
    ).astype(jnp.bfloat16)
    position = jnp.arange(row_block, dtype=jnp.int32)
    owner_local = lax.dynamic_slice_in_dim(owner, here * row_block, row_block)
    ordering = jnp.argsort(owner_local * row_block + position)
    inverse = jnp.argsort(ordering)
    home = lax.all_to_all(
        weights.reshape(n_dom, per_owner, members, members).astype(jnp.bfloat16),
        "dom",
        split_axis=0,
        concat_axis=0,
        tiled=True,
    ).astype(jnp.float32)
    native = jnp.take(home.reshape(row_block, members, members), inverse, axis=0)
    counts = lax.dynamic_slice_in_dim(obs_count, here * row_block, row_block)
    matrices = combined(native, counts)
    collected_entries = predicted_prior.reshape(
        members_on_shard, field_stack, member_total, quarter_part, row_block, grid_cells
    ).transpose(2, 0, 1, 3, 4, 5)
    gathered = lax.all_to_all(collected_entries, "mem", split_axis=0, concat_axis=1, tiled=True)
    analysed = jnp.einsum(
        "mflyx,ymn->nflyx", gathered[0], matrices, preferred_element_type=jnp.float32
    ).astype(jnp.bfloat16)
    returned = lax.all_to_all(analysed[None], "mem", split_axis=1, concat_axis=0, tiled=True)
    return returned.transpose(1, 2, 0, 3, 4, 5).reshape(
        members_on_shard, field_stack, levels, row_block, grid_cells
    )


def solution(mesh):
    in_specs = (
        P("mem", None, None, "dom", None),
        P(None, "dom", None),
        P(None, "dom", None),
        P(),
        P("dom", None, None),
        P(),
        P(),
    )
    out_specs = P("mem", None, None, "dom", None)
    return jax.shard_map(
        per_device, mesh=mesh, in_specs=in_specs, out_specs=out_specs, check_vma=False
    )
```

profile of v0, /device:TPU:0, one launch (start us, length us, event | category | flops | bytes accessed | tf_op | source)
XLA Modules:
  0.0 120.3 jit_solution(417325739760694209)
XLA Ops:
  0.0 1.8 %fusion.14 = (bf16[16,6,4,1,128]{4,3,2,1,0:T(2,128)(2,1)S(1)}, bf16[16,6,4,1,128]{4,3,2,1,0:T(2,128)(2,1)S(1)}) fusion(bf16[16,6,4,32,128]{4,3,2,1,0:T(8,128)(2,1)} %param.7), kind=kLoop, calls=%fused_computation.31 | loop fusion | bytes 393216 | tf_op jit(solution)/shard_map/slice | solution.py:15
  1.9 1.3 %collective-permute-start.1 = (bf16[16,6,4,1,128]{4,0,3,2,1:T(8,128)(2,1)S(1)}, bf16[16,6,4,1,128]{4,0,3,2,1:T(8,128)(2,1)}, u32[]{:S(2)}, u32[]{:S(2)}) collective-permute-start(bf16[16,6,4,1,128]{4,0,3,2,1:T(8,128)(2,1)S(1)} %copy.35), channel_id=1, source_target_pairs={{1,0},{2,1},{3,2},{4,3},{5,4},{6,5},{7,6},{9,8},{10,9},{11,10},{12... | collective-permute-start | bytes 294920 | tf_op jit(solution)/shard_map/ppermute | solution.py:17
  3.2 0.7 copy.34
  3.9 3.7 %collective-permute-start = (bf16[16,6,4,1,128]{4,0,3,2,1:T(8,128)(2,1)}, bf16[16,6,4,1,128]{4,0,3,2,1:T(8,128)(2,1)}, u32[]{:S(2)}, u32[]{:S(2)}) collective-permute-start(bf16[16,6,4,1,128]{4,0,3,2,1:T(8,128)(2,1)} %copy.34), channel_id=1, source_target_pairs={{0,1},{1,2},{2,3},{3,4},{4,5},{5,6},{6,7},{8,9},{9,10},{10,11},{11... | collective-permute-start | bytes 294920 | tf_op jit(solution)/shard_map/ppermute | solution.py:14
  7.5 2.1 %convert_element_type.39 = bf16[32,64,64]{2,1,0:T(8,128)(2,1)} convert(f32[32,64,64]{2,1,0:T(8,128)} %param.11) | non-fusion elementwise | flops 131072 | bytes 786432 | tf_op jit(solution)/shard_map/convert_element_type | solution.py:59
  9.6 2.1 %reshape.66 = bf16[8,2,8192]{2,1,0:T(2,128)(2,1)} reshape(bf16[8,4,64,64]{3,2,1,0:T(8,128)(2,1)} %bitcast.29) | data formatting | bytes 524288
  11.8 6.3 %all-to-all-start = ((bf16[8,2,8192]{2,1,0:T(2,128)(2,1)}), bf16[8,2,8192]{2,1,0:T(2,128)(2,1)S(1)}, u32[]{:S(2)}, u32[]{:S(2)}) async-start(bf16[8,2,8192]{2,1,0:T(2,128)(2,1)} %reshape.66), calls=%async_computation | async-start | bytes 524288 | tf_op jit(solution)/shard_map/all_to_all | solution.py:58
  18.1 0.0 collective-permute-done.1
  18.1 1.0 copy.26
  19.2 0.0 collective-permute-done
  19.2 1.0 copy.24
  20.2 2.2 %maximum_convert_fusion = f32[16,6,4,34,128]{4,3,1,0,2:T(8,128)S(1)} fusion(bf16[16,6,4,1,128]{4,3,1,0,2:T(2,128)(2,1)S(1)} %copy.26, bf16[16,6,4,1,128]{4,3,1,0,2:T(2,128)(2,1)S(1)} %copy.24, bf16[16,6,4,32,128]{4,3,2,1,0:T(8,128)(2,1)S(1)} %copy-done.1), kind=kLoop, calls=%fused_computation.4 | loop fusion | flops 10027008 | bytes 10027008 | tf_op jit(solution)/shard_map/convert_element_type | solution.py:42
  22.4 0.0 copy-start.2
  22.4 0.0 copy-start.3
  22.5 0.0 copy-start.4
  22.5 1.0 slice.30
  23.5 8.7 %fusion = bf16[4,16,6,1,32,128]{5,4,2,1,3,0:T(8,128)(2,1)} fusion(f32[4,32,128]{2,1,0:T(8,128)S(1)} %copy-done.2, f32[4,32,128]{2,1,0:T(8,128)S(1)} %copy-done.3, f32[16,6,4,32,128]{4,3,1,0,2:T(8,128)S(1)} %slice.30, f32[16,6,4,34,128]{4,3,1,0,2:T(8,128)S(1)} %maximum_convert_fusion, f32[6]{0:T(128)S(1)} %copy-done.4), kind=kLoop, calls=%fused_computation.7 | loop fusion | flops 23592960 | bytes 22151192 | tf_op jit(solution)/shard_map/transpose | solution.py:70
  32.2 4.0 %all-to-all-start.1 = ((bf16[4,16,6,1,32,128]{5,4,2,1,3,0:T(8,128)(2,1)}), bf16[4,16,6,1,32,128]{5,4,2,1,3,0:T(8,128)(2,1)S(1)}, u32[]{:S(2)}, u32[]{:S(2)}) async-start(bf16[4,16,6,1,32,128]{5,4,2,1,3,0:T(8,128)(2,1)} %fusion), calls=%async_computation.1 | async-start | bytes 6291456 | tf_op jit(solution)/shard_map/all_to_all | solution.py:71
  36.3 0.1 iota_add_fusion
  36.4 1.7 %sort.31 = (s32[32]{0:T(128)}, s32[32]{0:T(128)S(1)}) sort(s32[32]{0:T(128)S(1)} %iota_add_fusion, s32[32]{0:T(128)S(1)} %iota.27), dimensions={0}, to_apply=%region_0.1 | sort | flops 160 | bytes 512 | tf_op jit(solution)/shard_map/jit(argsort)/sort | solution.py:56
  38.0 1.7 %sort.32 = (s32[32]{0:T(128)}, s32[32]{0:T(128)S(1)}) sort(s32[32]{0:T(128)S(1)} %get-tuple-element.7, s32[32]{0:T(128)S(1)} %iota.28), dimensions={0}, to_apply=%region_1.2 | sort | flops 160 | bytes 512 | tf_op jit(solution)/shard_map/jit(argsort)/sort | solution.py:57
  39.7 0.1 broadcast_subtract_fusion
  39.9 1.2 reshape.67
  41.0 2.1 %bitcast_convert_fusion = f32[32,64,64]{2,1,0:T(8,128)} fusion(bf16[8,4,64,64]{3,2,1,0:T(8,128)(2,1)} %reshape.67), kind=kLoop, calls=%fused_computation.12 | loop fusion | flops 131072 | bytes 786432 | tf_op jit(solution)/shard_map/reshape | solution.py:65
  43.2 2.9 %gather_fusion = f32[32,64,64]{2,1,0:T(8,128)} fusion(f32[32,64,64]{2,1,0:T(8,128)} %bitcast_convert_fusion, s32[1024]{0:T(1024)S(1)} %pad_clamp_fusion), kind=kCustom, calls=%fused_computation | custom fusion | bytes 1048704 | tf_op jit(solution)/shard_map/jit(_take)/gather | solution.py:65
  46.1 1.5 %fusion.1 = f32[32,64]{1,0:T(8,128)S(1)} fusion(f32[32,64,64]{2,1,0:T(8,128)} %gather_fusion, f32[32]{0:T(128)S(1)} %get-tuple-element.10, f32[64,64]{1,0:T(8,128)S(1)} %fusion.11, f32[32]{0:T(128)S(1)} %get-tuple-element.9, pred[32]{0:T(512)(128)(4,1)S(1)} %compare_and_fusion), kind=kLoop, calls=%fused_computation.10 | loop fusion | flops 653312 | bytes 549152 | tf_op jit(solution)/shard_map/reduce_sum | solution.py:29
  47.6 25.5 %all-to-all-done.1 = bf16[4,16,6,1,32,128]{5,4,2,1,3,0:T(8,128)(2,1)S(1)} async-done(((bf16[4,16,6,1,32,128]{5,4,2,1,3,0:T(8,128)(2,1)}), bf16[4,16,6,1,32,128]{5,4,2,1,3,0:T(8,128)(2,1)S(1)}, u32[]{:S(2)}, u32[]{:S(2)}) %all-to-all-start.1) | async-done | bytes 3145760 | tf_op jit(solution)/shard_map/all_to_all | solution.py:71
  73.1 2.0 %copy.27 = bf16[4,16,6,1,32,128]{5,1,0,2,4,3:T(8,128)(2,1)S(1)} copy(bf16[4,16,6,1,32,128]{5,4,2,1,3,0:T(8,128)(2,1)S(1)} %all-to-all-done.1) | data formatting | bytes 6291456 | tf_op jit(solution)/shard_map/all_to_all | solution.py:71
  75.1 1.3 %convert_bitcast_fusion = bf16[1,64,6,1,32,128]{5,1,2,4,3,0:T(8,128)(2,1)S(1)} fusion(bf16[64,6,32,128]{3,0,1,2:T(8,128)(2,1)S(1)} %bitcast.28, f32[32,64,64]{2,1,0:T(8,128)S(1)} %copy-done, f32[32,64]{1,0:T(8,128)S(1)} %broadcast_multiply_fusion, f32[32]{0:T(128)S(1)} %get-tuple-element.10, f32[64,64]{1,0:T(8,128)S(1)} %fusion.11, ...), kind=kOutput, calls=%fused_computation.6 | convolution fusion | flops 203816960 | bytes 6840608 | tf_op jit(solution)/shard_map/mflyx,ymn->nflyx/dot_general | solution.py:72
  76.5 2.0 %copy.29 = bf16[1,64,6,1,32,128]{5,4,3,2,0,1:T(8,128)(2,1)S(1)} copy(bf16[1,64,6,1,32,128]{5,1,2,4,3,0:T(8,128)(2,1)S(1)} %convert_bitcast_fusion) | data formatting | bytes 6291456 | tf_op jit(solution)/shard_map/broadcast_in_dim | solution.py:75
  78.5 39.2 %all_to_all.26 = bf16[1,64,6,1,32,128]{5,4,3,2,0,1:T(8,128)(2,1)S(1)} all-to-all(bf16[1,64,6,1,32,128]{5,4,3,2,0,1:T(8,128)(2,1)S(1)} %copy.29), channel_id=1, replica_groups=mesh['mem'=4,'dom'=8] {'mem'}, dimensions={1} | all-to-all | bytes 6291456 | tf_op jit(solution)/shard_map/all_to_all | solution.py:75
  117.7 2.6 %copy.39 = bf16[4,16,6,1,32,128]{5,4,0,2,1,3:T(8,128)(2,1)} copy(bf16[4,16,6,1,32,128]{5,4,2,1,0,3:T(8,128)(2,1)S(1)} %bitcast.27) | data formatting | bytes 6291456 | tf_op jit(solution)/shard_map/all_to_all | solution.py:75
  (20 shorter events, 0.1 us)
Async XLA Ops:
  0.0 20.2 %copy-start.1 = (bf16[16,6,4,32,128]{4,3,2,1,0:T(8,128)(2,1)S(1)}, bf16[16,6,4,32,128]{4,3,2,1,0:T(8,128)(2,1)}, u32[]{:S(2)}) copy-start(bf16[16,6,4,32,128]{4,3,2,1,0:T(8,128)(2,1)} %param.7) | copy-start | bytes 9437188
  1.9 16.2 %collective-permute-start.1 = (bf16[16,6,4,1,128]{4,0,3,2,1:T(8,128)(2,1)S(1)}, bf16[16,6,4,1,128]{4,0,3,2,1:T(8,128)(2,1)}, u32[]{:S(2)}, u32[]{:S(2)}) collective-permute-start(bf16[16,6,4,1,128]{4,0,3,2,1:T(8,128)(2,1)S(1)} %copy.35), channel_id=1, source_target_pairs={{1,0},{2,1},{3,2},{4,3},{5,4},{6,5},{7,6},{9,8},{10,9},{11,10},{12... | collective-permute-start | bytes 294920 | tf_op jit(solution)/shard_map/ppermute | solution.py:17
  3.9 15.3 %collective-permute-start = (bf16[16,6,4,1,128]{4,0,3,2,1:T(8,128)(2,1)}, bf16[16,6,4,1,128]{4,0,3,2,1:T(8,128)(2,1)}, u32[]{:S(2)}, u32[]{:S(2)}) collective-permute-start(bf16[16,6,4,1,128]{4,0,3,2,1:T(8,128)(2,1)} %copy.34), channel_id=1, source_target_pairs={{0,1},{1,2},{2,3},{3,4},{4,5},{5,6},{6,7},{8,9},{9,10},{10,11},{11... | collective-permute-start | bytes 294920 | tf_op jit(solution)/shard_map/ppermute | solution.py:14
  11.8 20.5 %all-to-all-start = ((bf16[8,2,8192]{2,1,0:T(2,128)(2,1)}), bf16[8,2,8192]{2,1,0:T(2,128)(2,1)S(1)}, u32[]{:S(2)}, u32[]{:S(2)}) async-start(bf16[8,2,8192]{2,1,0:T(2,128)(2,1)} %reshape.66), calls=%async_computation | async-start | bytes 524288 | tf_op jit(solution)/shard_map/all_to_all | solution.py:58
  22.4 1.0 copy-start.2
  22.4 1.0 copy-start.3
  22.5 1.0 copy-start.4
  32.2 4.0 %copy-start.6 = (s32[256]{0:T(256)S(1)}, s32[256]{0:T(256)}, u32[]{:S(2)}) copy-start(s32[256]{0:T(256)} %param.13) | copy-start | bytes 3076
  32.2 7.5 %copy-start.5 = (s32[256]{0:T(256)S(1)}, s32[256]{0:T(256)}, u32[]{:S(2)}) copy-start(s32[256]{0:T(256)} %param.12) | copy-start | bytes 3076
  32.2 40.9 %all-to-all-start.1 = ((bf16[4,16,6,1,32,128]{5,4,2,1,3,0:T(8,128)(2,1)}), bf16[4,16,6,1,32,128]{5,4,2,1,3,0:T(8,128)(2,1)S(1)}, u32[]{:S(2)}, u32[]{:S(2)}) async-start(bf16[4,16,6,1,32,128]{5,4,2,1,3,0:T(8,128)(2,1)} %fusion), calls=%async_computation.1 | async-start | bytes 6291456 | tf_op jit(solution)/shard_map/all_to_all | solution.py:71
  73.1 2.0 %copy-start = (f32[32,64,64]{2,1,0:T(8,128)S(1)}, f32[32,64,64]{2,1,0:T(8,128)}, u32[]{:S(2)}) copy-start(f32[32,64,64]{2,1,0:T(8,128)} %gather_fusion) | copy-start | bytes 1572868
where the time goes:
time: 121 us; the launch traced here: 120 us
  blocking collectives  39.2 us (32%)
  waiting for transfers between devices  25.5 us (21%)
  other arithmetic  20.3 us (17%)
  local copies, waits for them, and re-layouts  18.5 us (15%)
  starting transfers between devices  15.3 us (13%)
  matrix products  1.32 us (1%)
    all_to_all x1, blocking collectives, per_device(): lax.all_to_all(analysed[None], 'mem', split_axis=1, concat_axis=0, tiled=...  39.2 us
    all_to_all x1, waiting for transfers between devices, per_device(): lax.all_to_all(collected_entries, 'mem', split_axis=0, concat_axis=1, til...  25.5 us
    transpose x1, other arithmetic, per_device(): collected_entries = predicted_prior.reshape(members_on_shard, field_stack...  8.72 us
    all_to_all x1, starting transfers between devices, per_device(): lax.all_to_all(weights.reshape(n_dom, per_owner, members, members).astype...  6.34 us
    unnamed x18, local copies, waits for them, and re-layouts  4.06 us
    all_to_all x1, starting transfers between devices, per_device(): lax.all_to_all(collected_entries, 'mem', split_axis=0, concat_axis=1, til...  4.02 us
    ppermute x1, starting transfers between devices, with_halo(): lax.ppermute(lax.slice_in_dim(block, block.shape[dim] - width, None, axis...  3.66 us
    gather x1, local copies, waits for them, and re-layouts, per_device(): jnp.take(home.reshape(row_block, members, members), inverse, axis=0)  2.87 us
  transfers between devices with their start and end apart: 4, of which 1 were waited for; matrix products, arithmetic and copies ran while one was open for 25% of the time, Pallas kernels for 0%

commit v1 on v0

v1 whole, which is shorter than its diff:
```python
import functools

import jax
import jax.numpy as jnp
from jax import lax
from jax.experimental import pallas as pl
from jax.experimental.pallas import tpu as pltpu
from jax.sharding import PartitionSpec as P

OBS_HALF = 8
GROUP = 16
STEP = 4
MESH = pl.DeviceIdType.MESH


def partner(me, count, step):
    if count == 4:
        return (me + 1 - 2 * (me % 2), (me + 2) % 4, 3 - me)[step - 1]
    return (me + step) % count


def sender(me, count, step):
    return partner(me, count, step) if count == 4 else (me + count - step) % count


def kernel(
    n_mem,
    n_dom,
    state,
    wind_x,
    wind_y,
    viscosity,
    weights,
    obs_count,
    owner,
    out,
    raw,
    low,
    high,
    fore,
    done,
    block_diag,
    stacked,
    weight_in,
    weight_out,
    home,
    wx,
    wy,
    sem_fwd_send,
    sem_fwd_recv,
    sem_own,
    sem_halo_send,
    sem_halo_recv,
    sem_ret_send,
    sem_ret_recv,
    sem_own_out,
    sem_w_send,
    sem_w_recv,
    sem_in,
):
    me = lax.axis_index("mem")
    here = lax.axis_index("dom")
    local, fields, _, rows, cells = state.shape
    members = local * n_mem
    per_owner = rows // n_dom
    groups = rows // GROUP

    weights_copy = pltpu.make_async_copy(weights, weight_in, sem_in.at[0])
    wx_copy = pltpu.make_async_copy(wind_x.at[me], wx, sem_in.at[1])
    wy_copy = pltpu.make_async_copy(wind_y.at[me], wy, sem_in.at[2])
    weights_copy.start()
    wx_copy.start()
    wy_copy.start()

    barrier = pltpu.get_barrier_semaphore()
    for step in range(1, n_mem):
        pl.semaphore_signal(
            barrier, inc=1, device_id=(partner(me, n_mem, step), here), device_id_type=MESH
        )

    def greet(step, carry):
        pl.semaphore_signal(
            barrier, inc=1, device_id=(me, (here + step) % n_dom), device_id_type=MESH
        )
        return carry

    lax.fori_loop(1, n_dom, greet, 0)
    pl.semaphore_wait(barrier, n_mem - 1 + n_dom - 1)

    def forward(step, field):
        to = partner(me, n_mem, step)
        return pltpu.make_async_remote_copy(
            src_ref=state.at[:, field, to],
            dst_ref=raw.at[field, pl.ds(me * local, local)],
            send_sem=sem_fwd_send.at[step - 1, field],
            recv_sem=sem_fwd_recv.at[step - 1, field],
            device_id=(to, here),
            device_id_type=MESH,
        )

    def own(field):
        return pltpu.make_async_copy(
            state.at[:, field, me], raw.at[field, pl.ds(me * local, local)], sem_own.at[field]
        )

    def halo_up(field):
        return pltpu.make_async_remote_copy(
            src_ref=raw.at[field, :, pl.ds(rows - GROUP, GROUP)],
            dst_ref=low.at[field],
            send_sem=sem_halo_send.at[0, field],
            recv_sem=sem_halo_recv.at[0, field],
            device_id=(me, (here + 1) % n_dom),
            device_id_type=MESH,
        )

    def halo_down(field):
        return pltpu.make_async_remote_copy(
            src_ref=raw.at[field, :, pl.ds(0, GROUP)],
            dst_ref=high.at[field],
            send_sem=sem_halo_send.at[1, field],
            recv_sem=sem_halo_recv.at[1, field],
            device_id=(me, (here + n_dom - 1) % n_dom),
            device_id_type=MESH,
        )

    def back(step, field):
        to = partner(me, n_mem, step)
        return pltpu.make_async_remote_copy(
            src_ref=done.at[field, pl.ds(to * local, local)],
            dst_ref=out.at[:, field, me],
            send_sem=sem_ret_send.at[step - 1, field],
            recv_sem=sem_ret_recv.at[step - 1, field],
            device_id=(to, here),
            device_id_type=MESH,
        )

    def own_out(field):
        return pltpu.make_async_copy(
            done.at[field, pl.ds(me * local, local)], out.at[:, field, me], sem_own_out.at[field]
        )

    def weight_to(step):
        to = (here + step) % n_dom
        return pltpu.make_async_remote_copy(
            src_ref=weight_out.at[pl.ds(to * per_owner, per_owner)],
            dst_ref=home.at[pl.ds(here * per_owner, per_owner)],
            send_sem=sem_w_send.at[step],
            recv_sem=sem_w_recv.at[step],
            device_id=(me, to),
            device_id_type=MESH,
        )

    def send_field(field, carry):
        for step in range(1, n_mem):
            forward(step, field).start()
        own(field).start()
        return carry

    lax.fori_loop(0, fields, send_field, 0)

    weights_copy.wait()

    def narrow(block, carry):
        weight_out[block] = weight_in[block].astype(jnp.bfloat16)
        return carry

    lax.fori_loop(0, rows, narrow, 0)

    def send_weight(step, carry):
        weight_to(step).start()
        return carry

    lax.fori_loop(1, n_dom, send_weight, 0)
    own_weight = pltpu.make_async_copy(
        weight_out.at[pl.ds(here * per_owner, per_owner)],
        home.at[pl.ds(here * per_owner, per_owner)],
        sem_in.at[3],
    )
    own_weight.start()

    @pl.when(here == 0)
    def _():
        low[...] = jnp.zeros_like(low)

    @pl.when(here == n_dom - 1)
    def _():
        high[...] = jnp.zeros_like(high)

    def share_edges(field):
        own(field).wait()
        for step in range(1, n_mem):
            forward(step, field).wait_recv()

        @pl.when(here < n_dom - 1)
        def _():
            halo_up(field).start()

        @pl.when(here > 0)
        def _():
            halo_down(field).start()

    own_weight.wait()

    def take_weight(step, carry):
        weight_to(step).wait_recv()
        return carry

    lax.fori_loop(1, n_dom, take_weight, 0)

    row_id = lax.broadcasted_iota(jnp.int32, (members, members), 0)
    col_id = lax.broadcasted_iota(jnp.int32, (members, members), 1)
    eye = (row_id == col_id).astype(jnp.float32)
    eye_narrow = eye.astype(jnp.bfloat16)
    base = here * rows

    def combine(block, carry):
        mine = owner[base + block]

        def count(other, total):
            return total + jnp.where(owner[base + other] == mine, 1, 0)

        rank = lax.fori_loop(0, block, count, 0)
        weight = home[mine * per_owner + rank].astype(jnp.float32)
        number = jnp.full((members, members), obs_count[base + block], jnp.int32).astype(
            jnp.float32
        )
        gain = number / (number + OBS_HALF)
        mixing = (1.0 - gain) * eye + gain * weight
        square = (
            mixing - jnp.mean(mixing, axis=0, keepdims=True) + 1.0 / members
        ).astype(jnp.bfloat16)
        flipped = lax.dot_general(
            square, eye_narrow, (((0,), (0,)), ((), ())), preferred_element_type=jnp.float32
        )
        group = block // GROUP
        place = block % GROUP
        stacked[group, pl.ds(place, members, stride=GROUP), pl.ds(0, members)] = flipped
        return carry

    lax.fori_loop(0, rows, combine, 0)

    wide = members * GROUP
    spread_row = lax.broadcasted_iota(jnp.int32, (members, wide), 0)
    spread_col = lax.broadcasted_iota(jnp.int32, (members, wide), 1)
    spread = ((spread_col >> 4) == spread_row).astype(jnp.bfloat16)
    piece = 64
    mask = (
        (lax.broadcasted_iota(jnp.int32, (piece, wide), 0) & (GROUP - 1))
        == (lax.broadcasted_iota(jnp.int32, (piece, wide), 1) & (GROUP - 1))
    )

    for group in range(groups):

        def widen(part, carry, group=group):
            start = pl.multiple_of(part * piece, piece)
            lines = stacked[group, pl.ds(start, piece), pl.ds(0, members)].astype(jnp.bfloat16)
            full = jnp.dot(lines, spread, preferred_element_type=jnp.float32)
            block_diag[group, pl.ds(start, piece)] = jnp.where(mask, full, 0.0).astype(
                jnp.bfloat16
            )
            return carry

        lax.fori_loop(0, wide // piece, widen, 0)

    wx_copy.wait()
    wy_copy.wait()
    share_edges(0)

    flat = STEP * rows
    line = lax.broadcasted_iota(jnp.int32, (flat, cells), 0) & (rows - 1)
    cell = lax.broadcasted_iota(jnp.int32, (flat, cells), 1)
    first_line, last_line = line == 0, line == rows - 1
    first_cell, last_cell = cell == 0, cell == cells - 1
    blank = jnp.zeros((STEP, rows - GROUP, cells), jnp.float32)

    def work(field, carry):
        @pl.when(field < fields - 1)
        def _():
            share_edges(field + 1)

        @pl.when(here > 0)
        def _():
            halo_up(field).wait_recv()

        @pl.when(here < n_dom - 1)
        def _():
            halo_down(field).wait_recv()

        number = viscosity[field]
        along = jnp.broadcast_to(wx[...][None], (STEP, rows, cells)).reshape(flat, cells)
        across = jnp.broadcast_to(wy[...][None], (STEP, rows, cells)).reshape(flat, cells)

        def stencil(part, inner):
            which = pl.ds(part * STEP, STEP)
            middle = raw[field, which].astype(jnp.float32).reshape(flat, cells)
            under = low[field, which].astype(jnp.float32).reshape(STEP * GROUP, cells)
            over = high[field, which].astype(jnp.float32).reshape(STEP * GROUP, cells)
            under = pltpu.roll(under, STEP * GROUP - (GROUP - 1), 0).reshape(STEP, GROUP, cells)
            over = pltpu.roll(over, GROUP - 1, 0).reshape(STEP, GROUP, cells)
            under = jnp.concatenate([under, blank], axis=1).reshape(flat, cells)
            over = jnp.concatenate([blank, over], axis=1).reshape(flat, cells)
            lower = jnp.where(first_line, under, pltpu.roll(middle, 1, 0))
            upper = jnp.where(last_line, over, pltpu.roll(middle, flat - 1, 0))
            west = jnp.where(first_cell, 0.0, pltpu.roll(middle, 1, 1))
            east = jnp.where(last_cell, 0.0, pltpu.roll(middle, cells - 1, 1))
            ensemble = upper + lower + east + west - 4.0 * middle
            carried = along * (east - west) + across * (upper - lower)
            prior = middle + number * ensemble - 0.5 * carried
            fore[which] = prior.astype(jnp.bfloat16).reshape(STEP, rows, cells)
            return inner

        lax.fori_loop(0, members // STEP, stencil, 0)

        for group in range(groups):
            lines = pl.ds(group * GROUP, GROUP)
            prior = fore[:, lines].reshape(wide, cells)

            def transform(part, inner, group=group, lines=lines, prior=prior):
                start = pl.multiple_of(part * 256, 256)
                result = jnp.dot(
                    block_diag[group, pl.ds(start, 256)],
                    prior,
                    preferred_element_type=jnp.float32,
                )
                many = 256 // GROUP
                done[field, pl.ds(part * many, many), lines] = result.astype(
                    jnp.bfloat16
                ).reshape(many, GROUP, cells)
                return inner

            lax.fori_loop(0, wide // 256, transform, 0)

        for step in range(1, n_mem):
            back(step, field).start()
        own_out(field).start()
        return carry

    lax.fori_loop(0, fields, work, 0)

    def finish_weight(step, carry):
        weight_to(step).wait_send()
        return carry

    lax.fori_loop(1, n_dom, finish_weight, 0)

    def finish(field, carry):
        for step in range(1, n_mem):
            forward(step, field).wait_send()

        @pl.when(here < n_dom - 1)
        def _():
            halo_up(field).wait_send()

        @pl.when(here > 0)
        def _():
            halo_down(field).wait_send()

        for step in range(1, n_mem):
            back(step, field).wait_send()
            back(step, field).wait_recv()
        own_out(field).wait()
        return carry

    lax.fori_loop(0, fields, finish, 0)


def per_device(state, wind_x, wind_y, viscosity_numbers, weights, obs_count, owner):
    n_mem = lax.axis_size("mem")
    n_dom = lax.axis_size("dom")
    local, fields, levels, rows, cells = state.shape
    members = local * n_mem
    groups = rows // GROUP
    wide = members * GROUP
    anywhere = pl.BlockSpec(memory_space=pl.ANY)
    scalars = pl.BlockSpec(memory_space=pltpu.SMEM)
    dma = pltpu.SemaphoreType.DMA
    return pl.pallas_call(
        functools.partial(kernel, n_mem, n_dom),
        out_shape=jax.ShapeDtypeStruct(state.shape, state.dtype),
        in_specs=[anywhere, anywhere, anywhere, scalars, anywhere, scalars, scalars],
        out_specs=anywhere,
        scratch_shapes=[
            pltpu.VMEM((fields, members, rows, cells), jnp.bfloat16),
            pltpu.VMEM((fields, members, GROUP, cells), jnp.bfloat16),
            pltpu.VMEM((fields, members, GROUP, cells), jnp.bfloat16),
            pltpu.VMEM((members, rows, cells), jnp.bfloat16),
            pltpu.VMEM((fields, members, rows, cells), jnp.bfloat16),
            pltpu.VMEM((groups, wide, wide), jnp.bfloat16),
            pltpu.VMEM((groups, wide, 128), jnp.float32),
            pltpu.VMEM((rows, members, members), jnp.float32),
            pltpu.VMEM((rows, members, members), jnp.bfloat16),
            pltpu.VMEM((rows, members, members), jnp.bfloat16),
            pltpu.VMEM((rows, cells), jnp.float32),
            pltpu.VMEM((rows, cells), jnp.float32),
            dma((n_mem - 1, fields)),
            dma((n_mem - 1, fields)),
            dma((fields,)),
            dma((2, fields)),
            dma((2, fields)),
            dma((n_mem - 1, fields)),
            dma((n_mem - 1, fields)),
            dma((fields,)),
            dma((n_dom,)),
            dma((n_dom,)),
            dma((4,)),
        ],
        compiler_params=pltpu.CompilerParams(
            collective_id=0, has_side_effects=True, vmem_limit_bytes=48 * 1024 * 1024
        ),
        cost_estimate=pl.CostEstimate(
            flops=4 * wide * wide * groups * fields * cells // 2,
            bytes_accessed=4 * state.size,
            transcendentals=0,
        ),
    )(state, wind_x, wind_y, viscosity_numbers, weights, obs_count, owner)


def solution(mesh):
    in_specs = (
        P("mem", None, None, "dom", None),
        P(None, "dom", None),
        P(None, "dom", None),
        P(),
        P("dom", None, None),
        P(),
        P(),
    )
    out_specs = P("mem", None, None, "dom", None)
    return jax.shard_map(
        per_device, mesh=mesh, in_specs=in_specs, out_specs=out_specs, check_vma=False
    )
```

time: 121 us -> 86.3 us (0.71)
  the two profiles are of different devices: /device:TPU:0 before, /device:TPU:17 now
where the time goes in v1:
time: 86.3 us; the launch traced here: 86 us
  Pallas kernels  79.4 us (92%)
  local copies, waits for them, and re-layouts  6.58 us (8%)
    pallas_call x1, Pallas kernels, per_device(): pl.pallas_call(functools.partial(kernel, n_mem, n_dom), out_shape=jax.Sha...  79.4 us
    unnamed x13, local copies, waits for them, and re-layouts  6.58 us

profile of v1, /device:TPU:17, one launch (start us, length us, event | category | flops | bytes accessed | tf_op | source)
XLA Modules:
  0.0 86.0 jit_solution(6219179403637885207)
XLA Ops:
  0.0 0.0 copy-start
  0.0 1.2 %copy-done = f32[32,64,64]{2,1,0:T(8,128)S(1)} copy-done((f32[32,64,64]{2,1,0:T(8,128)S(1)}, f32[32,64,64]{2,1,0:T(8,128)}, u32[]{:S(2)}) %copy-start) | copy-done | bytes 524312
  1.2 0.0 copy-start.1
  1.2 0.8 copy-done.1
  2.1 0.0 copy-start.2
  2.1 0.8 copy-done.2
  2.9 0.0 copy-start.3
  2.9 0.7 copy-done.3
  3.6 0.0 copy-start.4
  3.6 0.7 copy-done.4
  4.3 0.0 copy-start.5
  4.3 0.7 copy-done.5
  4.9 79.4 %shard_map.73 = bf16[16,6,4,32,128]{4,3,2,1,0:T(8,128)(2,1)S(1)} custom-call(bf16[16,6,4,32,128]{4,3,2,1,0:T(8,128)(2,1)} %state.1, f32[4,32,128]{2,1,0:T(8,128)S(1)} %copy-done.1, f32[4,32,128]{2,1,0:T(8,128)S(1)} %copy-done.2, f32[6]{0:T(128)S(1)} %copy-done.5, f32[32,64,64]{2,1,0:T(8,128)S(1)} %copy-done, s32[256]{0:T(256)S(1)} %copy-done.3, s32[256]{0:T(256)S(1)} %copy-done.4), custom_call_target="tpu_custom_call" | custom-call | flops 3221225472 | bytes 6291456 | tf_op jit(solution)/shard_map/pallas_call | solution.py:377
  84.4 1.7 %copy.9 = bf16[16,6,4,32,128]{4,3,2,1,0:T(8,128)(2,1)} copy(bf16[16,6,4,32,128]{4,3,2,1,0:T(8,128)(2,1)S(1)} %shard_map.73) | data formatting | bytes 6291456
Async XLA Ops:
  0.0 1.2 %copy-start = (f32[32,64,64]{2,1,0:T(8,128)S(1)}, f32[32,64,64]{2,1,0:T(8,128)}, u32[]{:S(2)}) copy-start(f32[32,64,64]{2,1,0:T(8,128)} %weights.1) | copy-start | bytes 1572868
  1.2 0.8 copy-start.1
  2.1 0.8 copy-start.2
  2.9 0.7 copy-start.3
  3.6 0.7 copy-start.4
  4.3 0.7 copy-start.5

commit v2 on v1

--- a/solution.py
+++ b/solution.py
@@ -29,10 +29,10 @@
     state,
     wind_x,
     wind_y,
-    viscosity,
+    viscosity_in,
     weights,
-    obs_count,
-    owner,
+    obs_count_in,
+    owner_in,
     out,
     raw,
     low,
@@ -46,6 +46,9 @@
     home,
     wx,
     wy,
+    viscosity,
+    obs_count,
+    owner,
     sem_fwd_send,
     sem_fwd_recv,
     sem_own,
@@ -68,9 +71,12 @@
     weights_copy = pltpu.make_async_copy(weights, weight_in, sem_in.at[0])
     wx_copy = pltpu.make_async_copy(wind_x.at[me], wx, sem_in.at[1])
     wy_copy = pltpu.make_async_copy(wind_y.at[me], wy, sem_in.at[2])
-    weights_copy.start()
-    wx_copy.start()
-    wy_copy.start()
+    viscosity_copy = pltpu.make_async_copy(viscosity_in, viscosity, sem_in.at[4])
+    count_copy = pltpu.make_async_copy(obs_count_in, obs_count, sem_in.at[5])
+    owner_copy = pltpu.make_async_copy(owner_in, owner, sem_in.at[6])
+    inputs = (weights_copy, wx_copy, wy_copy, viscosity_copy, count_copy, owner_copy)
+    for copy in inputs:
+        copy.start()
 
     barrier = pltpu.get_barrier_semaphore()
     for step in range(1, n_mem):
@@ -200,6 +206,8 @@
             halo_down(field).start()
 
     own_weight.wait()
+    for copy in inputs[1:]:
+        copy.wait()
 
     def take_weight(step, carry):
         weight_to(step).wait_recv()
@@ -262,8 +270,6 @@
 
         lax.fori_loop(0, wide // piece, widen, 0)
 
-    wx_copy.wait()
-    wy_copy.wait()
     share_edges(0)
 
     flat = STEP * rows
@@ -372,12 +378,12 @@
     groups = rows // GROUP
     wide = members * GROUP
     anywhere = pl.BlockSpec(memory_space=pl.ANY)
-    scalars = pl.BlockSpec(memory_space=pltpu.SMEM)
+    stay = pl.BlockSpec(memory_space=pltpu.HBM)
     dma = pltpu.SemaphoreType.DMA
     return pl.pallas_call(
         functools.partial(kernel, n_mem, n_dom),
         out_shape=jax.ShapeDtypeStruct(state.shape, state.dtype),
-        in_specs=[anywhere, anywhere, anywhere, scalars, anywhere, scalars, scalars],
+        in_specs=[stay] * 7,
         out_specs=anywhere,
         scratch_shapes=[
             pltpu.VMEM((fields, members, rows, cells), jnp.bfloat16),
@@ -392,6 +398,9 @@
             pltpu.VMEM((rows, members, members), jnp.bfloat16),
             pltpu.VMEM((rows, cells), jnp.float32),
             pltpu.VMEM((rows, cells), jnp.float32),
+            pltpu.SMEM(viscosity_numbers.shape, jnp.float32),
+            pltpu.SMEM(obs_count.shape, jnp.int32),
+            pltpu.SMEM(owner.shape, jnp.int32),
             dma((n_mem - 1, fields)),
             dma((n_mem - 1, fields)),
             dma((fields,)),
@@ -402,7 +411,7 @@
             dma((fields,)),
             dma((n_dom,)),
             dma((n_dom,)),
-            dma((4,)),
+            dma((7,)),
         ],
         compiler_params=pltpu.CompilerParams(
             collective_id=0, has_side_effects=True, vmem_limit_bytes=48 * 1024 * 1024
@@ -412,7 +421,12 @@
             bytes_accessed=4 * state.size,
             transcendentals=0,
         ),
-    )(state, wind_x, wind_y, viscosity_numbers, weights, obs_count, owner)
+    )(
+        *(
+            pltpu.with_memory_space_constraint(array, pltpu.HBM)
+            for array in (state, wind_x, wind_y, viscosity_numbers, weights, obs_count, owner)
+        )
+    )
 
 
 def solution(mesh):

time: 86.3 us -> 80.6 us (0.934)
  local copies, waits for them, and re-layouts: 6.58 us -> 1.67 us
    unnamed x13 -> x1, local copies, waits for them, and re-layouts: 6.58 us -> 1.67 us
where the time goes in v2:
time: 80.6 us; the launch traced here: 80.5 us
  Pallas kernels  78.8 us (98%)
  local copies, waits for them, and re-layouts  1.67 us (2%)
    pallas_call x1, Pallas kernels, per_device(): pl.pallas_call(functools.partial(kernel, n_mem, n_dom), out_shape=jax.Sha...  78.8 us
    unnamed x1, local copies, waits for them, and re-layouts  1.67 us

profile of v2, /device:TPU:17, one launch (start us, length us, event | category | flops | bytes accessed | tf_op | source)
XLA Modules:
  0.0 80.5 jit_solution(7602438146110631618)
XLA Ops:
  0.0 78.8 %shard_map.73 = bf16[16,6,4,32,128]{4,3,2,1,0:T(8,128)(2,1)S(1)} custom-call(bf16[16,6,4,32,128]{4,3,2,1,0:T(8,128)(2,1)} %state.1, f32[4,32,128]{2,1,0:T(8,128)} %wind_x.1, f32[4,32,128]{2,1,0:T(8,128)} %wind_y.1, f32[6]{0:T(128)} %viscosity_in.1, f32[32,64,64]{2,1,0:T(8,128)} %weights.1, s32[256]{0:T(256)} %obs_count_in.1, s32[256]{0:T(256)} %owner_in.1), custom_call_target="tpu_custom_call" | custom-call | flops 3221225472 | bytes 6291456 | tf_op jit(solution)/shard_map/pallas_call | solution.py:383
  78.8 1.7 %copy.9 = bf16[16,6,4,32,128]{4,3,2,1,0:T(8,128)(2,1)} copy(bf16[16,6,4,32,128]{4,3,2,1,0:T(8,128)(2,1)S(1)} %shard_map.73) | data formatting | bytes 6291456

commit v3 on v2

--- a/solution.py
+++ b/solution.py
@@ -60,6 +60,8 @@
     sem_w_send,
     sem_w_recv,
     sem_in,
+    sem_met,
+    sem_all,
 ):
     me = lax.axis_index("mem")
     here = lax.axis_index("dom")
@@ -79,19 +81,30 @@
         copy.start()
 
     barrier = pltpu.get_barrier_semaphore()
+    gate = me == 0
     for step in range(1, n_mem):
-        pl.semaphore_signal(
-            barrier, inc=1, device_id=(partner(me, n_mem, step), here), device_id_type=MESH
-        )
-
-    def greet(step, carry):
-        pl.semaphore_signal(
-            barrier, inc=1, device_id=(me, (here + step) % n_dom), device_id_type=MESH
-        )
-        return carry
-
-    lax.fori_loop(1, n_dom, greet, 0)
-    pl.semaphore_wait(barrier, n_mem - 1 + n_dom - 1)
+        to = partner(me, n_mem, step)
+
+        @pl.when(to != 0)
+        def _(to=to):
+            pl.semaphore_signal(barrier, inc=1, device_id=(to, here), device_id_type=MESH)
+
+    @pl.when(jnp.logical_not(gate))
+    def _():
+        pl.semaphore_wait(barrier, n_mem - 1)
+        pl.semaphore_signal(sem_met, inc=1, device_id=(0, here), device_id_type=MESH)
+
+    @pl.when(gate)
+    def _():
+        pl.semaphore_wait(sem_met, n_mem - 1)
+
+        def greet(step, carry):
+            pl.semaphore_signal(
+                barrier, inc=1, device_id=(0, (here + step) % n_dom), device_id_type=MESH
+            )
+            return carry
+
+        lax.fori_loop(1, n_dom, greet, 0)
 
     def forward(step, field):
         to = partner(me, n_mem, step)
@@ -171,6 +184,16 @@
         return carry
 
     lax.fori_loop(0, rows, narrow, 0)
+
+    @pl.when(gate)
+    def _():
+        pl.semaphore_wait(barrier, n_dom - 1)
+        for other in range(1, n_mem):
+            pl.semaphore_signal(sem_all, inc=1, device_id=(other, here), device_id_type=MESH)
+
+    @pl.when(jnp.logical_not(gate))
+    def _():
+        pl.semaphore_wait(sem_all, 1)
 
     def send_weight(step, carry):
         weight_to(step).start()
@@ -412,6 +435,8 @@
             dma((n_dom,)),
             dma((n_dom,)),
             dma((7,)),
+            pltpu.SemaphoreType.REGULAR,
+            pltpu.SemaphoreType.REGULAR,
         ],
         compiler_params=pltpu.CompilerParams(
             collective_id=0, has_side_effects=True, vmem_limit_bytes=48 * 1024 * 1024

time: 80.6 us -> 83.3 us (1.033)
  Pallas kernels: 78.8 us -> 81.5 us
    pallas_call x1, Pallas kernels: 78.8 us -> 81.5 us  [per_device(): pl.pallas_call(functools.partial(kernel, n_mem, n_dom), out_shape=jax.Sha...]
where the time goes in v3:
time: 83.3 us; the launch traced here: 83.2 us
  Pallas kernels  81.5 us (98%)
  local copies, waits for them, and re-layouts  1.67 us (2%)
    pallas_call x1, Pallas kernels, per_device(): pl.pallas_call(functools.partial(kernel, n_mem, n_dom), out_shape=jax.Sha...  81.5 us
    unnamed x1, local copies, waits for them, and re-layouts  1.67 us

profile of v3, /device:TPU:17, one launch (start us, length us, event | category | flops | bytes accessed | tf_op | source)
XLA Modules:
  0.0 83.2 jit_solution(12034733420532989684)
XLA Ops:
  0.0 81.5 %shard_map.73 = bf16[16,6,4,32,128]{4,3,2,1,0:T(8,128)(2,1)S(1)} custom-call(bf16[16,6,4,32,128]{4,3,2,1,0:T(8,128)(2,1)} %state.1, f32[4,32,128]{2,1,0:T(8,128)} %wind_x.1, f32[4,32,128]{2,1,0:T(8,128)} %wind_y.1, f32[6]{0:T(128)} %viscosity_in.1, f32[32,64,64]{2,1,0:T(8,128)} %weights.1, s32[256]{0:T(256)} %obs_count_in.1, s32[256]{0:T(256)} %owner_in.1), custom_call_target="tpu_custom_call" | custom-call | flops 3221225472 | bytes 6291456 | tf_op jit(solution)/shard_map/pallas_call | solution.py:406
  81.5 1.7 %copy.9 = bf16[16,6,4,32,128]{4,3,2,1,0:T(8,128)(2,1)} copy(bf16[16,6,4,32,128]{4,3,2,1,0:T(8,128)(2,1)S(1)} %shard_map.73) | data formatting | bytes 6291456

commit v4 on v3

--- a/solution.py
+++ b/solution.py
@@ -49,6 +49,7 @@
     viscosity,
     obs_count,
     owner,
+    place_of,
     sem_fwd_send,
     sem_fwd_recv,
     sem_own,
@@ -106,6 +107,7 @@
 
         lax.fori_loop(1, n_dom, greet, 0)
 
+
     def forward(step, field):
         to = partner(me, n_mem, step)
         return pltpu.make_async_remote_copy(
@@ -207,6 +209,7 @@
     )
     own_weight.start()
 
+
     @pl.when(here == 0)
     def _():
         low[...] = jnp.zeros_like(low)
@@ -228,9 +231,22 @@
         def _():
             halo_down(field).start()
 
-    own_weight.wait()
     for copy in inputs[1:]:
         copy.wait()
+    base = here * rows
+
+    def locate(block, carry):
+        mine = owner[base + block]
+
+        def count(other, total):
+            return total + jnp.where(owner[base + other] == mine, 1, 0)
+
+        place_of[block] = mine * per_owner + lax.fori_loop(0, block, count, 0)
+        return carry
+
+    lax.fori_loop(0, rows, locate, 0)
+    share_edges(0)
+    own_weight.wait()
 
     def take_weight(step, carry):
         weight_to(step).wait_recv()
@@ -242,16 +258,9 @@
     col_id = lax.broadcasted_iota(jnp.int32, (members, members), 1)
     eye = (row_id == col_id).astype(jnp.float32)
     eye_narrow = eye.astype(jnp.bfloat16)
-    base = here * rows
 
     def combine(block, carry):
-        mine = owner[base + block]
-
-        def count(other, total):
-            return total + jnp.where(owner[base + other] == mine, 1, 0)
-
-        rank = lax.fori_loop(0, block, count, 0)
-        weight = home[mine * per_owner + rank].astype(jnp.float32)
+        weight = home[place_of[block]].astype(jnp.float32)
         number = jnp.full((members, members), obs_count[base + block], jnp.int32).astype(
             jnp.float32
         )
@@ -268,7 +277,8 @@
         stacked[group, pl.ds(place, members, stride=GROUP), pl.ds(0, members)] = flipped
         return carry
 
-    lax.fori_loop(0, rows, combine, 0)
+    lax.fori_loop(0, rows, combine, 0, unroll=4)
+    share_edges(1)
 
     wide = members * GROUP
     spread_row = lax.broadcasted_iota(jnp.int32, (members, wide), 0)
@@ -293,7 +303,6 @@
 
         lax.fori_loop(0, wide // piece, widen, 0)
 
-    share_edges(0)
 
     flat = STEP * rows
     line = lax.broadcasted_iota(jnp.int32, (flat, cells), 0) & (rows - 1)
@@ -303,10 +312,6 @@
     blank = jnp.zeros((STEP, rows - GROUP, cells), jnp.float32)
 
     def work(field, carry):
-        @pl.when(field < fields - 1)
-        def _():
-            share_edges(field + 1)
-
         @pl.when(here > 0)
         def _():
             halo_up(field).wait_recv()
@@ -362,6 +367,11 @@
         for step in range(1, n_mem):
             back(step, field).start()
         own_out(field).start()
+
+        @pl.when(field < fields - 2)
+        def _():
+            share_edges(field + 2)
+
         return carry
 
     lax.fori_loop(0, fields, work, 0)
@@ -424,6 +434,7 @@
             pltpu.SMEM(viscosity_numbers.shape, jnp.float32),
             pltpu.SMEM(obs_count.shape, jnp.int32),
             pltpu.SMEM(owner.shape, jnp.int32),
+            pltpu.SMEM((rows,), jnp.int32),
             dma((n_mem - 1, fields)),
             dma((n_mem - 1, fields)),
             dma((fields,)),

time: 83.3 us -> 75.5 us (0.906)
  the two profiles are of different devices: /device:TPU:17 before, /device:TPU:0 now
where the time goes in v4:
time: 75.5 us; the launch traced here: 75.4 us
  Pallas kernels  73.7 us (98%)
  local copies, waits for them, and re-layouts  1.67 us (2%)
    pallas_call x1, Pallas kernels, per_device(): pl.pallas_call(functools.partial(kernel, n_mem, n_dom), out_shape=jax.Sha...  73.7 us
    unnamed x1, local copies, waits for them, and re-layouts  1.67 us

profile of v4, /device:TPU:0, one launch (start us, length us, event | category | flops | bytes accessed | tf_op | source)
XLA Modules:
  0.0 75.4 jit_solution(14784610571435600735)
XLA Ops:
  0.0 73.7 %shard_map.73 = bf16[16,6,4,32,128]{4,3,2,1,0:T(8,128)(2,1)S(1)} custom-call(bf16[16,6,4,32,128]{4,3,2,1,0:T(8,128)(2,1)} %state.1, f32[4,32,128]{2,1,0:T(8,128)} %wind_x.1, f32[4,32,128]{2,1,0:T(8,128)} %wind_y.1, f32[6]{0:T(128)} %viscosity_in.1, f32[32,64,64]{2,1,0:T(8,128)} %weights.1, s32[256]{0:T(256)} %obs_count_in.1, s32[256]{0:T(256)} %owner_in.1), custom_call_target="tpu_custom_call" | custom-call | flops 3221225472 | bytes 6291456 | tf_op jit(solution)/shard_map/pallas_call | solution.py:416
  73.7 1.7 %copy.9 = bf16[16,6,4,32,128]{4,3,2,1,0:T(8,128)(2,1)} copy(bf16[16,6,4,32,128]{4,3,2,1,0:T(8,128)(2,1)S(1)} %shard_map.73) | data formatting | bytes 6291456
